TPU v7x, 256 devices: a whole 4x4x8 slice. The times are simulated.
256 devices in a mesh: tm: 32 (over y, z_hi, core), batch: 8 (over x, z_lo).
Axes of the slice: x: 4, y: 4, z: 8 (z_hi: 4, z_lo: 2; z = z_hi * 2 + z_lo), core: 2. Of those that a mesh axis runs over, the one named last changes fastest.
Arguments:
- features: bfloat16 [8, 2048, 128, 128], P('batch', 'tm'), may hold values from -6 to 6
- kernel_one: bfloat16 [3, 3, 128, 128], replicated, may hold values from -0.1875 to 0.1875
- proj_weight: bfloat16 [512, 1024], P(None, 'tm'), may hold values from -0.25 to 0.25
- upstream: bfloat16 [8, 1024, 64, 1024], P('batch', 'tm'), may hold values from -6 to 6
Outputs:
- projected: bfloat16 [8, 1024, 64, 1024], P('batch', 'tm')
- grad_features: bfloat16 [8, 2048, 128, 128], P('batch', 'tm')
- grad_kernel_one: float32 [3, 3, 128, 128], replicated
- grad_proj: float32 [512, 1024], P(None, 'tm')
All inputs are finite; a program needn't handle non-finite values.
Results may differ from a plain program's by a relative error of at most 0.0049.
Values may be sent and summed in bfloat16 or wider, within the bound.
A program may use at most 128 MiB of HBM per device.

v0:
```python
import math

import jax
import jax.numpy as jnp
from jax import lax
from jax.sharding import PartitionSpec as P


def extended(block, sides, width):
    for axis, dim in sides:
        count = lax.axis_size(axis)
        forward = [(i, i + 1) for i in range(count - 1)]
        backward = [(target, source) for source, target in forward]
        low = lax.ppermute(
            lax.slice_in_dim(block, block.shape[dim] - width, None, axis=dim), axis, forward
        )
        high = lax.ppermute(lax.slice_in_dim(block, 0, width, axis=dim), axis, backward)
        block = jnp.concatenate([low, block, high], axis=dim)
    return block


def conv_rows(padded, kernel):
    return lax.conv_general_dilated(
        padded,
        kernel,
        (1, 1),
        ((0, 0), (1, 1)),
        dimension_numbers=("NHWC", "HWIO", "NHWC"),
        preferred_element_type=jnp.float32,
    )


def flipped(kernel):
    return jnp.transpose(jnp.flip(kernel, (0, 1)), (0, 1, 3, 2))


def silu_slope(values):
    sig = jax.nn.sigmoid(values)
    return sig * (1.0 + values * (1.0 - sig))


def kernel_grad(padded, grad):
    batch_rows, frames, mels, chans = grad.shape
    wider = jnp.pad(padded, ((0, 0), (0, 0), (1, 1), (0, 0)))
    flat_grad = grad.reshape(-1, chans)
    rows_out = []
    for i in range(3):
        cols_out = []
        for j in range(3):
            piece = wider[:, i : i + frames, j : j + mels, :].reshape(-1, chans)
            cols_out.append(
                lax.dot_general(
                    piece, flat_grad, (((0,), (0,)), ((), ())), preferred_element_type=jnp.float32
                )
            )
        rows_out.append(jnp.stack(cols_out))
    return jnp.stack(rows_out)


def body(features, kernel_one, proj_weight, upstream):
    batch_rows, frames, mels, chans = features.shape
    filters = upstream.shape[3]
    shard_count = lax.axis_size("tm")
    scale = 1.0 / math.sqrt(batch_rows * lax.axis_size("batch") * frames * shard_count * mels)
    feat_pad = extended(features, (("tm", 1),), 1)
    pre_one = conv_rows(feat_pad, kernel_one)
    hidden_two = (features.astype(jnp.float32) + jax.nn.silu(pre_one)).astype(jnp.bfloat16)
    packed = (
        hidden_two.reshape(batch_rows, frames // 2, 2, mels // 2, 2, chans)
        .transpose(0, 1, 3, 2, 4, 5)
        .reshape(-1, 4 * chans)
    )
    cotangent = upstream.reshape(-1, filters)
    weight_full = lax.all_gather(proj_weight, "tm", axis=1, tiled=True)
    projected = jnp.dot(packed, weight_full, preferred_element_type=jnp.float32).astype(
        jnp.bfloat16
    )
    grad_packed = lax.dot_general(
        cotangent, weight_full, (((1,), (1,)), ((), ())), preferred_element_type=jnp.float32
    )
    grad_hidden_two = (
        grad_packed.reshape(batch_rows, frames // 2, mels // 2, 2, 2, chans)
        .transpose(0, 1, 3, 2, 4, 5)
        .reshape(batch_rows, frames, mels, chans)
    )
    grad_pre_one = (grad_hidden_two * silu_slope(pre_one)).astype(jnp.bfloat16)
    grad_pad = extended(grad_pre_one, (("tm", 1),), 1)
    grad_features = (grad_hidden_two + conv_rows(grad_pad, flipped(kernel_one))).astype(
        jnp.bfloat16
    )
    part_one = kernel_grad(feat_pad, grad_pre_one)
    share = lax.psum_scatter(
        lax.dot_general(
            cotangent, packed, (((0,), (0,)), ((), ())), preferred_element_type=jnp.float32
        ),
        "tm",
        scatter_dimension=0,
        tiled=True,
    )
    grad_proj = lax.psum(share.T, "batch") * scale
    total_one = lax.psum(part_one, ("tm", "batch"))
    return (projected.reshape(upstream.shape), grad_features, total_one * scale, grad_proj)


def solution(mesh):
    placed = (P("batch", "tm", None, None), P(), P(None, "tm"), P("batch", "tm", None, None))
    return jax.shard_map(
        body,
        mesh=mesh,
        in_specs=placed,
        out_specs=(P("batch", "tm", None, None), P("batch", "tm", None, None), P(), P(None, "tm")),
        check_vma=False,
    )
```

profile of v0, /device:TPU:8, one launch (start us, length us, event | category | flops | bytes accessed | tf_op | source)
XLA Modules:
  0.0 507.8 jit_solution(5901509793981179253)
XLA Ops:
  7.2 3.3 copy.41
  10.5 1.9 collective-permute-start
  12.4 7.5 %collective-permute-start.1 = (bf16[1,1,128,128]{2,3,1,0:T(8,128)(2,1)S(1)}, bf16[1,1,128,128]{2,3,1,0:T(8,128)(2,1)S(1)}, u32[]{:S(2)}, u32[]{:S(2)}) collective-permute-start(bf16[1,1,128,128]{2,3,1,0:T(8,128)(2,1)S(1)} %get-tuple-element.23), channel_id=1, source_target_pairs={{8,0},{16,8},{24,16},{32,24},{40,32},{48,40},{56,48},{64,56},{72,6... | collective-permute-start | bytes 98312 | tf_op jit(solution)/shard_map/ppermute | solution.py:17
  21.6 2.4 pad_maximum_fusion
  23.9 3.1 copy.71
  28.2 6.2 %add_multiply_fusion = (f32[64,8,17,128]{3,1,2,0:T(8,128)S(1)}, f32[64,8,17,128]{3,1,2,0:T(8,128)S(1)}) fusion(pred[8,17]{0,1:T(8,128)(4,1)S(1)} %copy-done.10, bf16[3,3,128,128]{3,2,1,0:T(8,128)(2,1)S(1)} %copy-done, bf16[66,1,7,2,128]{4,2,3,0,1:T(8,128)(2,1)S(1)} %slice.61, bf16[66,1,8,17,128]{4,2,3,0,1:T(8,128)(2,1)S(1)} %copy.46), kind=kOutput, calls=%fused_computation.9 | convolution fusion | flops 2584645632 | bytes 11742344 | tf_op jit(solution)/shard_map/conv_general_dilated | solution.py:23
  35.2 2.6 slice.63
  40.8 3.4 copy.85
  44.3 2.2 reshape.80
  46.5 5.2 %convolution_bitcast_fusion = f32[1024,512]{0,1:T(8,128)S(1)} fusion(bf16[2048,512]{1,0:T(8,128)(2,1)} %reshape.80, bf16[2048,1024]{1,0:T(8,128)(2,1)} %bitcast.200), kind=kOutput, calls=%fused_computation.72 | convolution fusion | flops 2147483648 | bytes 8388608 | tf_op jit(solution)/shard_map/dot_general | solution.py:93
  51.6 1.9 copy.67
  53.6 18.5 %all-gather.2.cloned.1.call-done = bf16[512,1024]{0,1:T(8,128)(2,1)} async-done(((bf16[512,32]{0,1:T(8,128)(2,1)}), bf16[512,1024]{0,1:T(8,128)(2,1)}) %all-gather.2.cloned.1.call-update) | async-done | bytes 1048592 | tf_op jit(solution)/shard_map/all_gather | solution.py:74
  73.7 4.2 fusion.25
  77.9 3.9 copy.50
  81.8 2.5 fusion.8
  85.0 2.2 collective-permute-start.2
  87.1 6.8 %collective-permute-start.3 = (bf16[1,1,128,128]{3,2,1,0:T(8,128)(2,1)S(1)}, bf16[1,1,128,128]{3,2,1,0:T(8,128)(2,1)S(1)}, u32[]{:S(2)}, u32[]{:S(2)}) collective-permute-start(bf16[1,1,128,128]{3,2,1,0:T(8,128)(2,1)S(1)} %get-tuple-element.21), channel_id=1, source_target_pairs={{8,0},{16,8},{24,16},{32,24},{40,32},{48,40},{56,48},{64,56},{72,6... | collective-permute-start | bytes 98312 | tf_op jit(solution)/shard_map/ppermute | solution.py:17
  104.6 6.0 %convolution_convert_fusion = bf16[2048,1024]{1,0:T(8,128)(2,1)} fusion(bf16[2048,512]{1,0:T(8,128)(2,1)} %reshape.80, bf16[512,1024]{0,1:T(8,128)(2,1)S(1)} %copy-done.9), kind=kOutput, calls=%fused_computation.23 | convolution fusion | flops 2149580800 | bytes 7340032 | tf_op jit(solution)/shard_map/dot_general | solution.py:75
  113.2 5.4 %broadcast_select_fusion = f32[64,8,17,128]{3,1,2,0:T(8,128)S(1)} fusion(pred[8,17]{0,1:T(8,128)(4,1)S(1)} %copy-done.10, bf16[3,3,128,128]{3,2,1,0:T(8,128)(2,1)S(1)} %copy-done, bf16[66,1,7,2,128]{4,2,3,0,1:T(8,128)(2,1)S(1)} %slice.66, bf16[66,1,8,17,128]{4,2,3,0,1:T(8,128)(2,1)S(1)} %copy.55), kind=kOutput, calls=%fused_computation.36 | convolution fusion | flops 2575732736 | bytes 7285896 | tf_op jit(solution)/shard_map/conv_general_dilated | solution.py:23
  121.6 4.0 fusion.6
  125.7 39.6 %reduce-scatter.4.cloned.1.call-done = f32[32,512]{1,0:T(8,128)} async-done(((f32[1024,512]{1,0:T(8,128)}), f32[32,512]{1,0:T(8,128)}) %reduce-scatter.4.cloned.1.call-update) | async-done | bytes 65552
  167.0 252.2 %all-reduce.4.cloned.1.call-done = f32[3,3,128,128]{3,2,1,0:T(8,128)} async-done(((f32[3,3,128,128]{3,2,1,0:T(8,128)}), f32[3,3,128,128]{3,2,1,0:T(8,128)}) %all-reduce.4.cloned.1.call-update) | async-done | bytes 589840 | tf_op jit(solution)/shard_map/psum | solution.py:101
  419.1 1.9 broadcast_multiply_fusion
  421.1 78.3 %all-reduce.6.cloned.1.call-done = f32[512,32]{1,0:T(8,128)} async-done(((f32[512,32]{1,0:T(8,128)}), f32[512,32]{1,0:T(8,128)}) %all-reduce.6.cloned.1.call-update) | async-done | bytes 65552 | tf_op jit(solution)/shard_map/psum | solution.py:100
  (65 shorter events, 28.2 us)
Async XLA Ops:
  7.2 20.7 %copy-start = (bf16[3,3,128,128]{3,2,1,0:T(8,128)(2,1)S(1)}, bf16[3,3,128,128]{3,2,1,0:T(8,128)(2,1)}, u32[]{:S(2)}) copy-start(bf16[3,3,128,128]{3,2,1,0:T(8,128)(2,1)} %param.5) | copy-start | bytes 884740
  7.2 65.0 %all-gather.2.cloned.1.call-start = ((), (), s32[]{:S(2)}) async-start(), calls=%async_computation.1 | async-start | bytes 1081344 | tf_op jit(solution)/shard_map/all_gather | solution.py:74
  10.5 13.5 %copy-start.6 = (bf16[1,64,128,128]{2,3,1,0:T(8,128)(2,1)}, bf16[1,64,128,128]{2,3,1,0:T(8,128)(2,1)S(1)}, u32[]{:S(2)}) copy-start(bf16[1,64,128,128]{2,3,1,0:T(8,128)(2,1)S(1)} %copy.41) | copy-start | bytes 6291460
  10.5 9.5 %collective-permute-start = (bf16[1,1,128,128]{2,3,1,0:T(8,128)(2,1)S(1)}, bf16[1,1,128,128]{2,3,1,0:T(8,128)(2,1)S(1)}, u32[]{:S(2)}, u32[]{:S(2)}) collective-permute-start(bf16[1,1,128,128]{2,3,1,0:T(8,128)(2,1)S(1)} %get-tuple-element.22), channel_id=1, source_target_pairs={{0,8},{8,16},{16,24},{24,32},{32,40},{40,48},{48,56},{56,64},{64,7... | collective-permute-start | bytes 98312 | tf_op jit(solution)/shard_map/ppermute | solution.py:14
  12.4 9.1 %collective-permute-start.1 = (bf16[1,1,128,128]{2,3,1,0:T(8,128)(2,1)S(1)}, bf16[1,1,128,128]{2,3,1,0:T(8,128)(2,1)S(1)}, u32[]{:S(2)}, u32[]{:S(2)}) collective-permute-start(bf16[1,1,128,128]{2,3,1,0:T(8,128)(2,1)S(1)} %get-tuple-element.23), channel_id=1, source_target_pairs={{8,0},{16,8},{24,16},{32,24},{40,32},{48,40},{56,48},{64,56},{72,6... | collective-permute-start | bytes 98312 | tf_op jit(solution)/shard_map/ppermute | solution.py:17
  20.0 145.2 %reduce-scatter.4.cloned.1.call-start = ((), (), s32[]{:S(2)}) async-start(), calls=%async_computation.4 | async-start | bytes 2162688
  27.5 0.7 copy-start.10
  37.8 1.6 copy-start.3
  53.6 365.5 %all-reduce.4.cloned.1.call-start = ((), (), s32[]{:S(2)}) async-start(), calls=%async_computation.2 | async-start | bytes 1179648 | tf_op jit(solution)/shard_map/psum | solution.py:101
  77.9 3.9 copy-start.5
  81.8 2.5 copy-start.1
  81.8 12.1 %copy-start.8 = (bf16[1,66,128,128]{2,3,1,0:T(8,128)(2,1)S(1)}, bf16[1,66,128,128]{2,3,1,0:T(8,128)(2,1)}, u32[]{:S(2)}) copy-start(bf16[1,66,128,128]{2,3,1,0:T(8,128)(2,1)} %get-tuple-element.18) | copy-start | bytes 6488068
  85.0 25.7 %collective-permute-start.2 = (bf16[1,1,128,128]{3,2,1,0:T(8,128)(2,1)}, bf16[1,1,128,128]{3,2,1,0:T(8,128)(2,1)S(1)}, u32[]{:S(2)}, u32[]{:S(2)}) collective-permute-start(bf16[1,1,128,128]{3,2,1,0:T(8,128)(2,1)} %get-tuple-element.20), channel_id=1, source_target_pairs={{0,8},{8,16},{16,24},{24,32},{32,40},{40,48},{48,56},{56,64},{64,7... | collective-permute-start | bytes 98312 | tf_op jit(solution)/shard_map/ppermute | solution.py:14
  87.1 23.5 %collective-permute-start.3 = (bf16[1,1,128,128]{3,2,1,0:T(8,128)(2,1)S(1)}, bf16[1,1,128,128]{3,2,1,0:T(8,128)(2,1)S(1)}, u32[]{:S(2)}, u32[]{:S(2)}) collective-permute-start(bf16[1,1,128,128]{3,2,1,0:T(8,128)(2,1)S(1)} %get-tuple-element.21), channel_id=1, source_target_pairs={{8,0},{16,8},{24,16},{32,24},{40,32},{48,40},{56,48},{64,56},{72,6... | collective-permute-start | bytes 98312 | tf_op jit(solution)/shard_map/ppermute | solution.py:17
  94.8 1.6 copy-start.7
  100.7 1.6 copy-start.4
  103.2 1.5 copy-start.9
  104.1 395.2 %all-reduce.6.cloned.1.call-start = ((), (), s32[]{:S(2)}) async-start(), calls=%async_computation.3 | async-start | bytes 524288 | tf_op jit(solution)/shard_map/psum | solution.py:100
  119.4 2.2 copy-start.2
Sparse Core Ops, SparseCore 0:
  20.1 51.9 all-gather.1
  76.0 89.2 reduce-scatter.3
  171.3 247.7 all-reduce.3
  421.8 77.4 all-reduce.5
where the time goes:
time: 518 us; the launch traced here: 508 us
  waiting for transfers between devices  390 us (75%)
  local copies, waits for them, and re-layouts  35.7 us (7%)
  matrix products  34.5 us (7%)
  starting transfers between devices  18.8 us (4%)
  other arithmetic  14.4 us (3%)
  between operations  14.4 us (3%)
    psum x1, waiting for transfers between devices, body(): total_one = lax.psum(part_one, ('tm', 'batch'))  252 us
    psum x1, waiting for transfers between devices, body(): grad_proj = lax.psum(share.T, 'batch') * scale  78.3 us
    unnamed x5, waiting for transfers between devices  39.7 us
    all_gather x1, waiting for transfers between devices, body(): weight_full = lax.all_gather(proj_weight, 'tm', axis=1, tiled=True)  18.5 us
    unnamed x28, local copies, waits for them, and re-layouts  16.9 us
    ppermute x2, starting transfers between devices, extended(): lax.ppermute(lax.slice_in_dim(block, 0, width, axis=dim), axis, backward)  14.3 us
    conv_general_dilated x2, matrix products, conv_rows(): lax.conv_general_dilated(padded, kernel, (1, 1), ((0, 0), (1, 1)), dimens...  11.5 us
  transfers between devices with their start and end apart: 8, of which 5 were waited for; matrix products, arithmetic and copies ran while one was open for 15% of the time, Pallas kernels for 0%

commit v1 on v0

v1 whole, which is shorter than its diff:
```python
import math

import jax
import jax.numpy as jnp
from jax import lax
from jax.experimental import pallas as pl
from jax.experimental.pallas import tpu as pltpu
from jax.sharding import PartitionSpec as P

BF = jnp.bfloat16
F32 = jnp.float32
MESH = pl.DeviceIdType.MESH


def dot(a, b):
    return jnp.dot(a, b, preferred_element_type=F32)


def place(dst, i, block):
    base = i * 512
    zero = jnp.zeros((128, 128), BF)
    dst[base : base + 128, 0:128] = block(1)
    dst[base : base + 128, 128:256] = block(0)
    dst[base + 128 : base + 256, 0:128] = block(2)
    dst[base + 128 : base + 256, 128:256] = block(1)
    dst[base + 256 : base + 384, 0:128] = block(0)
    dst[base + 256 : base + 384, 128:256] = zero
    dst[base + 384 : base + 512, 0:128] = zero
    dst[base + 384 : base + 512, 128:256] = block(2)


def kernel(
    scale, feat, kern, pw, up, proj_out, gf_out, gk_out, gp_out,
    fx, st, x4, y4, sl, pk, pkt, gh, ub, wt, wn, wf, wb, po, gfo, gt, dk,
    gps, r0, s1, r1, s2, r2, s3, r3,
    k0, ra, sb, rb, sc, rc, kd, ke,
    in_sem, pout_sem, fout_sem,
    hx_s, hx_r, hy_s, hy_r, wz_s, wz_r, wy_s, wy_r, wc_s, wc_r,
    g0_s, g0_r, g1_s, g1_r, g2_s, g2_r, g3_s, g3_r,
    ka_s, ka_r, kb_s, kb_r, kc_s, kc_r, kd_s, kd_r, ke_s, ke_r,
):
    tm = lax.axis_index("tm")
    bt = lax.axis_index("batch")
    core, zh, y = tm % 2, (tm // 2) % 4, tm // 8
    x, zl = bt // 2, bt % 2
    z = zh * 2 + zl
    xy = x * 4 + y

    def device(cx, cy, cz, cc):
        return {"tm": (cy * 4 + cz // 2) * 2 + cc, "batch": cx * 2 + cz % 2}

    def remote(src, dst, ssem, rsem, dev):
        return pltpu.make_async_remote_copy(
            src_ref=src, dst_ref=dst, send_sem=ssem, recv_sem=rsem,
            device_id=dev, device_id_type=MESH,
        )

    partner = device(x, y, z, 1 - core)
    left = {"tm": (tm + 31) % 32, "batch": bt}
    right = {"tm": (tm + 1) % 32, "batch": bt}

    def y_peer(d):
        return device(x, (y + d) % 4, z, core)

    def z_peer(d):
        return device(x, y, (z + d) % 8, core)

    def b_peer(d):
        return {"tm": tm, "batch": (bt + d) % 8}

    def xy_peer(d):
        return device((x + d // 4) % 4, (y + d % 4) % 4, z, core)

    feat_in = pltpu.make_async_copy(feat, fx, in_sem.at[0])
    up_in = pltpu.make_async_copy(up, ub, in_sem.at[1])
    feat_in.start()
    up_in.start()

    barrier = pltpu.get_barrier_semaphore()
    greet = [partner, left, right]
    greet += [z_peer(d) for d in range(1, 8)]
    greet += [b_peer(d) for d in range(1, 8)]
    greet += [xy_peer(d) for d in range(1, 16)]
    for dev in greet:
        pl.semaphore_signal(barrier, inc=1, device_id=dev, device_id_type=MESH)

    wt[y, zh, core] = pw[...].T
    for i in range(3):
        place(wf, i, lambda j: kern[i, j])
        place(wb, i, lambda j: kern[2 - i, 2 - j].T)

    row = lax.broadcasted_iota(jnp.int32, (512, 128), 0) % 64

    def build(k):
        st[8:1032, :] = fx[pl.ds(k * 8, 8)].reshape(1024, 128).astype(F32)
        at = pl.ds(k * 8 + 1, 8)
        x4[at, :, 0:128] = st[pl.ds(8, 512, stride=2), :].astype(BF).reshape(8, 64, 128)
        x4[at, :, 128:256] = st[pl.ds(9, 512, stride=2), :].astype(BF).reshape(8, 64, 128)
        low = jnp.where(row == 0, 0.0, st[pl.ds(7, 512, stride=2), :])
        x4[at, :, 256:384] = low.astype(BF).reshape(8, 64, 128)
        high = jnp.where(row == 63, 0.0, st[pl.ds(10, 512, stride=2), :])
        x4[at, :, 384:512] = high.astype(BF).reshape(8, 64, 128)

    feat_in.wait()
    build(0)
    build(7)

    pl.semaphore_wait(barrier, len(greet))

    side = 2 * zl - 1
    wz = [
        remote(
            wt.at[y, zh, core], wt.at[y, zh, core], wz_s.at[d - 1], wz_r.at[d - 1],
            device(x, y, (z + side * d + 8) % 8, core),
        )
        for d in range(1, 4)
    ]
    for copy in wz:
        copy.start()
    hx = [
        remote(x4.at[1], x4.at[65], hx_s.at[0], hx_r.at[0], left),
        remote(x4.at[64], x4.at[0], hx_s.at[1], hx_r.at[1], right),
    ]
    for copy in hx:
        copy.start()

    @pl.loop(1, 7)
    def _(k):
        build(k)

    def forward(k):
        t0 = k * 8
        lhs = jnp.concatenate([x4[pl.ds(t0 + i, 8)].reshape(512, 512) for i in range(3)], axis=1)
        pre = dot(lhs, wf[...])
        here = x4[pl.ds(t0 + 1, 8), :, 0:256].reshape(512, 256).astype(F32)
        sig = 0.5 * jnp.tanh(0.5 * pre) + 0.5
        act = pre * sig
        slope = (sig + act * (1.0 - sig)).reshape(4, 2, 64, 256)
        hidden = (here + act).astype(BF).reshape(4, 2, 64, 256)
        at = pl.ds(k * 4, 4)
        both = jnp.concatenate([hidden[:, 0], hidden[:, 1]], axis=-1)
        pk[at] = both
        sl[at, :, 0:256] = slope[:, 0]
        sl[at, :, 256:512] = slope[:, 1]
        pkt[:, pl.ds(pl.multiple_of(k * 256, 256), 256)] = both.reshape(256, 512).T

    @pl.loop(1, 4)
    def _(k):
        forward(k)

    for copy in wz:
        copy.wait()
    wy = [
        remote(wt.at[y, :, core], wt.at[y, :, core], wy_s.at[d - 1], wy_r.at[d - 1], y_peer(d))
        for d in range(1, 4)
    ]
    wc = [
        remote(
            wt.at[(y + 4 - d) % 4, :, core], wt.at[(y + 4 - d) % 4, :, core],
            wc_s.at[d], wc_r.at[d], partner,
        )
        for d in range(4)
    ]
    for copy in wy:
        copy.start()
    wc[0].start()

    @pl.loop(4, 7)
    def _(k):
        forward(k)

    for copy in hx:
        copy.wait()

    @pl.when(tm == 0)
    def _():
        x4[0] = jnp.zeros((64, 512), BF)

    @pl.when(tm == 31)
    def _():
        x4[65] = jnp.zeros((64, 512), BF)

    forward(0)
    forward(7)

    up_in.wait()
    order = [2, 1, 3, 0]
    g0 = {
        d: remote(
            gps.at[(y + d) % 4, :, 1 - core], r0.at[(y + d) % 4], g0_s.at[d], g0_r.at[d], partner
        )
        for d in order
    }
    g1 = {
        d: remote(s1.at[(y + d) % 4], r1.at[y], g1_s.at[d - 1], g1_r.at[d - 1], y_peer(d))
        for d in (1, 2, 3)
    }

    def proj_chunk(d):
        cols = pl.ds(pl.multiple_of(((y + d) % 4) * 256, 256), 256)
        part = dot(pkt[...], ub[:, :, cols].reshape(2048, 256))
        gps[(y + d) % 4] = part.astype(BF).T.reshape(4, 2, 32, 512)
        g0[d].start()

    def core_sum(d):
        g0[d].wait()
        yd = (y + d) % 4
        total = gps[yd, :, core].astype(F32) + r0[yd].astype(F32)
        if d == 0:
            r1[y] = total.astype(BF)
        else:
            s1[yd] = total.astype(BF)
            g1[d].start()

    def pass_on(d):
        wy[d - 1].wait()
        wc[d].start()

    proj_chunk(2)
    pass_on(1)
    proj_chunk(1)
    core_sum(2)
    pass_on(3)
    proj_chunk(3)
    core_sum(1)
    pass_on(2)
    proj_chunk(0)
    core_sum(3)

    for copy in wc:
        copy.wait()

    for yy in range(4):
        wn[:, yy * 256 : (yy + 1) * 256] = wt[yy].reshape(256, 512).T

    row3 = lax.broadcasted_iota(jnp.int32, (8, 64, 128), 1)

    def grads(k):
        at = pl.ds(k * 8, 8)
        gp = dot(ub[at].reshape(512, 1024), wt[...].reshape(1024, 512))
        gh[at] = gp.reshape(8, 64, 512)
        g = (gp * sl[at].reshape(512, 512)).astype(BF).reshape(8, 64, 512)
        gf = g.astype(F32)
        lows, highs = [], []
        for p in range(2):
            odd = gf[:, :, p * 256 + 128 : p * 256 + 256]
            even = gf[:, :, p * 256 : p * 256 + 128]
            lows.append(jnp.where(row3 == 0, 0.0, pltpu.roll(odd, 1, 1)).astype(BF))
            highs.append(jnp.where(row3 == 63, 0.0, pltpu.roll(even, 63, 1)).astype(BF))
        for t in range(8):
            for p in range(2):
                f = k * 16 + 1 + 2 * t + p
                y4[f, :, 0:256] = g[t, :, p * 256 : p * 256 + 256]
                y4[f, :, 256:384] = lows[p][t]
                y4[f, :, 384:512] = highs[p][t]
        rows = jnp.concatenate(
            [g[t, :, p * 256 : p * 256 + 256] for t in range(8) for p in range(2)], axis=0
        )
        gt[:, pl.ds(pl.multiple_of(k * 1024, 1024), 1024)] = rows.T

    grads(0)
    grads(3)
    hy = [
        remote(y4.at[1], y4.at[65], hy_s.at[0], hy_r.at[0], left),
        remote(y4.at[64], y4.at[0], hy_s.at[1], hy_r.at[1], right),
    ]
    for copy in hy:
        copy.start()
    core_sum(0)

    @pl.loop(1, 3)
    def _(k):
        grads(k)

    for copy in g1.values():
        copy.wait()
    total = r1[0].astype(F32)
    for yy in range(1, 4):
        total = total + r1[yy].astype(F32)
    s2[...] = total.astype(BF).reshape(4, 2, 16, 512)
    g2 = []
    for d in range(1, 8):
        zd = (z + d) % 8
        g2.append(remote(s2.at[zd // 2, zd % 2], r2.at[z], g2_s.at[d - 1], g2_r.at[d - 1], z_peer(d)))
    for copy in g2:
        copy.start()
    r2[z] = s2[zh, zl]

    @pl.loop(0, 3)
    def _(i):
        dk[i] = dot(gt[...], x4[pl.ds(i, 64)].reshape(4096, 512))

    for i in range(3):
        q0, q1 = dk[i, 0:128], dk[i, 128:256]
        parts = (
            q1[:, 0:128] + q0[:, 256:384],
            q0[:, 0:128] + q1[:, 128:256],
            q0[:, 128:256] + q1[:, 384:512],
        )
        for j in range(3):
            block = parts[j].astype(BF).reshape(8, 16, 128)
            n = (i * 3 + j) * 8
            if n < 36 < n + 8:
                k0[0, n:36] = block[: 36 - n]
                k0[1, 0 : n - 28] = block[36 - n :]
            else:
                k0[n // 36, n % 36 : n % 36 + 8] = block
    ka = remote(k0.at[1 - core], ra, ka_s.at[0], ka_r.at[0], partner)
    ka.start()

    for copy in g2:
        copy.wait()
    total = r2[0].astype(F32)
    for zz in range(1, 8):
        total = total + r2[zz].astype(F32)
    s3[...] = total.astype(BF)
    g3 = [remote(s3, r3.at[bt], g3_s.at[d - 1], g3_r.at[d - 1], b_peer(d)) for d in range(1, 8)]
    for copy in g3:
        copy.start()
    r3[bt] = s3[...]

    def backward(k):
        t0 = k * 8
        lhs = jnp.concatenate([y4[pl.ds(t0 + i, 8)].reshape(512, 512) for i in range(3)], axis=1)
        out = dot(lhs, wb[...])
        h = gh[pl.ds(k * 4, 4)]
        out = out + jnp.concatenate(
            [h[t, :, p * 256 : p * 256 + 256] for t in range(4) for p in range(2)], axis=0
        )
        st[pl.ds(8, 512, stride=2), :] = out[:, 0:128]
        st[pl.ds(9, 512, stride=2), :] = out[:, 128:256]
        gfo[pl.ds(t0, 8)] = st[8:1032, :].astype(BF).reshape(8, 128, 128)
        pltpu.make_async_copy(gfo.at[pl.ds(t0, 8)], gf_out.at[pl.ds(t0, 8)], fout_sem.at[k]).start()

    def project(k):
        po[pl.ds(k * 8, 8)] = (
            dot(pk[pl.ds(k * 8, 8)].reshape(512, 512), wn[...]).astype(BF).reshape(8, 64, 1024)
        )
        pltpu.make_async_copy(po.at[pl.ds(k * 8, 8)], proj_out.at[pl.ds(k * 8, 8)], pout_sem.at[k]).start()

    @pl.loop(1, 3)
    def _(k):
        backward(k)

    ka.wait()
    sb[0:12] = (k0[core].astype(F32) + ra[...].astype(F32)).astype(BF).reshape(12, 3, 16, 128)
    sb[12:16] = jnp.zeros((4, 3, 16, 128), BF)
    kb = []
    for d in range(1, 16):
        owner = ((x + d // 4) % 4) * 4 + (y + d % 4) % 4
        kb.append(remote(sb.at[owner], rb.at[xy], kb_s.at[d - 1], kb_r.at[d - 1], xy_peer(d)))
    for copy in kb:
        copy.start()
    rb[xy] = sb[xy]

    @pl.loop(3, 6)
    def _(k):
        backward(k)

    for copy in kb:
        copy.wait()
    total = rb[0].astype(F32)
    for n in range(1, 16):
        total = total + rb[n].astype(F32)
    sc[...] = total.astype(BF)
    kc = [remote(sc, rc.at[z], kc_s.at[d - 1], kc_r.at[d - 1], z_peer(d)) for d in range(1, 8)]
    for copy in kc:
        copy.start()
    rc[z] = sc[...]

    for copy in hy:
        copy.wait()

    @pl.when(tm == 0)
    def _():
        y4[0] = jnp.zeros((64, 512), BF)

    @pl.when(tm == 31)
    def _():
        y4[65] = jnp.zeros((64, 512), BF)

    backward(0)

    @pl.loop(6, 8)
    def _(k):
        backward(k)

    for copy in kc:
        copy.wait()
    total = rc[0].astype(F32)
    for zz in range(1, 8):
        total = total + rc[zz].astype(F32)
    kd[xy] = total.astype(BF)
    kdc = [
        remote(kd.at[xy], kd.at[xy], kd_s.at[d - 1], kd_r.at[d - 1], xy_peer(d)) for d in range(1, 16)
    ]
    for copy in kdc:
        copy.start()

    @pl.loop(0, 2)
    def _(k):
        project(k)

    for copy in kdc:
        copy.wait()
    kec = remote(kd, ke, ke_s.at[0], ke_r.at[0], partner)
    kec.start()

    @pl.loop(2, 4)
    def _(k):
        project(k)

    for copy in g3:
        copy.wait()
    for half in range(2):
        total = r3[half].astype(F32)
        for n in range(1, 4):
            total = total + r3[2 * n + half].astype(F32)
        gp_out[half * 16 : half * 16 + 16, :] = total * scale

    kec.wait()
    gk_out[core] = kd[0:12].astype(F32).reshape(36, 16, 128) * scale
    gk_out[1 - core] = ke[0:12].astype(F32).reshape(36, 16, 128) * scale

    @pl.loop(0, 8)
    def _(k):
        pltpu.make_async_copy(gfo.at[pl.ds(k * 8, 8)], gf_out.at[pl.ds(k * 8, 8)], fout_sem.at[k]).wait()

    @pl.loop(0, 4)
    def _(k):
        pltpu.make_async_copy(po.at[pl.ds(k * 8, 8)], proj_out.at[pl.ds(k * 8, 8)], pout_sem.at[k]).wait()


def vm(*shape, dtype=BF):
    return pltpu.VMEM(shape, dtype)


def body(features, kernel_one, proj_weight, upstream):
    scale = 1.0 / math.sqrt(8 * 2048 * 128)
    dma = pltpu.SemaphoreType.DMA
    counts = [2, 4, 8]
    counts += [2, 2, 2, 2, 3, 3, 3, 3, 4, 4]
    counts += [4, 4, 3, 3, 7, 7, 7, 7]
    counts += [1, 1, 15, 15, 7, 7, 15, 15, 1, 1]
    whole = pl.BlockSpec(memory_space=pltpu.VMEM)
    hbm = pl.BlockSpec(memory_space=pl.ANY)
    projected, grad_features, gk, gp = pl.pallas_call(
        lambda *refs: kernel(scale, *refs),
        out_shape=(
            jax.ShapeDtypeStruct((32, 64, 1024), BF),
            jax.ShapeDtypeStruct((64, 128, 128), BF),
            jax.ShapeDtypeStruct((2, 36, 16, 128), F32),
            jax.ShapeDtypeStruct((32, 512), F32),
        ),
        in_specs=[hbm, whole, whole, hbm],
        out_specs=(hbm, hbm, whole, whole),
        scratch_shapes=[
            vm(64, 128, 128),
            vm(1040, 128, dtype=F32),
            vm(66, 64, 512),
            vm(66, 64, 512),
            vm(32, 64, 512, dtype=F32),
            vm(32, 64, 512),
            vm(512, 2048),
            vm(32, 64, 512, dtype=F32),
            vm(32, 64, 1024),
            vm(4, 4, 2, 32, 512),
            vm(512, 1024),
            vm(1536, 256),
            vm(1536, 256),
            vm(32, 64, 1024),
            vm(64, 128, 128),
            vm(256, 4096),
            vm(3, 256, 512, dtype=F32),
            vm(4, 4, 2, 32, 512),
            vm(4, 4, 32, 512),
            vm(4, 4, 32, 512),
            vm(4, 4, 32, 512),
            vm(4, 2, 16, 512),
            vm(8, 16, 512),
            vm(16, 512),
            vm(8, 16, 512),
            vm(2, 36, 16, 128),
            vm(36, 16, 128),
            vm(16, 3, 16, 128),
            vm(16, 3, 16, 128),
            vm(3, 16, 128),
            vm(8, 3, 16, 128),
            vm(16, 3, 16, 128),
            vm(16, 3, 16, 128),
        ]
        + [dma((n,)) for n in counts],
        compiler_params=pltpu.CompilerParams(
            collective_id=0, has_side_effects=True, vmem_limit_bytes=60 * 1024 * 1024
        ),
    )(features[0], kernel_one, proj_weight, upstream[0])
    return (
        projected[None],
        grad_features[None],
        jnp.transpose(gk.reshape(3, 3, 128, 128), (0, 1, 3, 2)),
        gp.T,
    )


def solution(mesh):
    placed = (P("batch", "tm", None, None), P(), P(None, "tm"), P("batch", "tm", None, None))
    return jax.shard_map(
        body,
        mesh=mesh,
        in_specs=placed,
        out_specs=(P("batch", "tm", None, None), P("batch", "tm", None, None), P(), P(None, "tm")),
        check_vma=False,
    )
```

time: 518 us -> 72.1 us (0.14)
  the two profiles are of different devices: /device:TPU:8 before, /device:TPU:1 now
where the time goes in v1:
time: 72.1 us; the launch traced here: 71.9 us
  Pallas kernels  60.6 us (84%)
  local copies, waits for them, and re-layouts  10.7 us (15%)
    pallas_call x1, Pallas kernels, body(): pl.pallas_call(lambda *refs: kernel(scale, *refs), out_shape=(jax.ShapeDt...  60.6 us
    unnamed x8, local copies, waits for them, and re-layouts  8.54 us
    reshape x1, local copies, waits for them, and re-layouts, body(): gk.reshape(3, 3, 128, 128)  2.11 us

profile of v1, /device:TPU:1, one launch (start us, length us, event | category | flops | bytes accessed | tf_op | source)
XLA Modules:
  0.0 71.9 jit_solution(13754556620662295436)
XLA Ops:
  0.6 1.5 %copy.8.refs_2_ = bf16[512,32]{1,0:T(8,128)(2,1)} copy(bf16[512,32]{0,1:T(8,128)(2,1)} %param.6) | data formatting | bytes 65536 | tf_op args[2]
  2.1 60.6 %shard_map.75 = (bf16[32,64,1024]{2,1,0:T(8,128)(2,1)}, bf16[64,128,128]{2,1,0:T(8,128)(2,1)}, f32[2,36,16,128]{3,2,1,0:T(8,128)}, f32[32,512]{1,0:T(8,128)}) custom-call(bf16[64,128,128]{2,1,0:T(8,128)(2,1)} %bitcast.9, bf16[3,3,128,128]{3,2,1,0:T(8,128)(2,1)} %refs_1_.1, bf16[512,32]{1,0:T(8,128)(2,1)} %copy.8.refs_2_, bf16[32,64,1024]{2,1,0:T(8,128)(2,1)} %bitcast.7), custom_call_target="tpu_custom_call" | custom-call | tf_op jit(solution)/shard_map/pallas_call | solution.py:447
  62.8 2.1 %copy.9 = f32[3,3,128,128]{2,3,1,0:T(8,128)} copy(f32[3,3,128,128]{3,2,1,0:T(8,128)} %bitcast.12) | data formatting | bytes 1179648 | tf_op jit(solution)/shard_map/reshape | solution.py:500
  64.9 0.0 copy-start
  64.9 0.0 copy-start.1
  64.9 5.1 %copy.13 = bf16[1,32,64,1024]{3,2,1,0:T(8,128)(2,1)} copy(bf16[1,32,64,1024]{3,2,1,0:T(8,128)(2,1)} %bitcast.8) | data formatting | bytes 8388608
  69.9 0.0 copy-done
  70.0 1.3 %copy.14 = bf16[1,64,128,128]{3,2,1,0:T(8,128)(2,1)} copy(bf16[1,64,128,128]{3,2,1,0:T(8,128)(2,1)S(1)} %bitcast.10) | data formatting | bytes 4194304
  71.3 0.0 copy-done.1
  71.3 0.6 copy.15
Async XLA Ops:
  64.9 5.1 %copy-start = (bf16[64,128,128]{2,1,0:T(8,128)(2,1)S(1)}, bf16[64,128,128]{2,1,0:T(8,128)(2,1)}, u32[]{:S(2)}) copy-start(bf16[64,128,128]{2,1,0:T(8,128)(2,1)} %get-tuple-element.9) | copy-start | bytes 6291460
  64.9 6.4 %copy-start.1 = (f32[32,512]{1,0:T(8,128)S(1)}, f32[32,512]{1,0:T(8,128)}, u32[]{:S(2)}) copy-start(f32[32,512]{1,0:T(8,128)} %get-tuple-element.11) | copy-start | bytes 196612

commit v2 on v1

v2 whole, which is shorter than its diff:
```python
import math

import jax
import jax.numpy as jnp
from jax import lax
from jax.experimental import pallas as pl
from jax.experimental.pallas import tpu as pltpu
from jax.sharding import PartitionSpec as P

BF = jnp.bfloat16
F32 = jnp.float32
MESH = pl.DeviceIdType.MESH
EARLY = 4


def dot(a, b):
    return jnp.dot(a, b, preferred_element_type=F32)


def place(dst, i, block):
    base = i * 512
    zero = jnp.zeros((128, 128), BF)
    dst[base : base + 128, 0:128] = block(1)
    dst[base : base + 128, 128:256] = block(0)
    dst[base + 128 : base + 256, 0:128] = block(2)
    dst[base + 128 : base + 256, 128:256] = block(1)
    dst[base + 256 : base + 384, 0:128] = block(0)
    dst[base + 256 : base + 384, 128:256] = zero
    dst[base + 384 : base + 512, 0:128] = zero
    dst[base + 384 : base + 512, 128:256] = block(2)


def kernel(
    scale, feat, kern, pwt, up, proj_out, gf_out, gk_out, gp_out,
    st, x4, xta, xtb, y4c, y4w, sl, pk, pkt, gh, wt, wn, wf, wb,
    gps, r0, s1, r1, s2, r2, s3, r3, r4,
    k0, ra, sb, rb, sc, rc, kd, ke,
    in_sem,
    hx_s, hx_r, hy_s, hy_r, wz_s, wz_r, wy_s, wy_r, wc_s, wc_r,
    g0_s, g0_r, g1_s, g1_r, g2_s, g2_r, g3_s, g3_r, g4_s, g4_r,
    ka_s, ka_r, kb_s, kb_r, kc_s, kc_r, kd_s, kd_r, ke_s, ke_r,
):
    tm = lax.axis_index("tm")
    bt = lax.axis_index("batch")
    core, zh, y = tm % 2, (tm // 2) % 4, tm // 8
    x, zl = bt // 2, bt % 2
    z = zh * 2 + zl
    xy = x * 4 + y

    def device(cx, cy, cz, cc):
        return {"tm": (cy * 4 + cz // 2) * 2 + cc, "batch": cx * 2 + cz % 2}

    def remote(src, dst, ssem, rsem, dev):
        return pltpu.make_async_remote_copy(
            src_ref=src, dst_ref=dst, send_sem=ssem, recv_sem=rsem,
            device_id=dev, device_id_type=MESH,
        )

    partner = device(x, y, z, 1 - core)
    left = {"tm": (tm + 31) % 32, "batch": bt}
    right = {"tm": (tm + 1) % 32, "batch": bt}
    side = 2 * zl - 1

    def y_peer(d):
        return device(x, (y + d) % 4, z, core)

    def z_peer(d):
        return device(x, y, (z + d) % 8, core)

    def b_peer(d):
        return {"tm": tm, "batch": (bt + d) % 8}

    def xy_peer(d):
        return device((x + d // 4) % 4, (y + d % 4) % 4, z, core)

    def x_peer(d):
        return device((x + d) % 4, y, z, core)

    barrier = pltpu.get_barrier_semaphore()
    greet = [partner, left, right]
    greet += [z_peer(d) for d in range(1, 8)]
    greet += [b_peer(d) for d in range(1, 8)]
    greet += [xy_peer(d) for d in range(1, 16)]
    for dev in greet:
        pl.semaphore_signal(barrier, inc=1, device_id=dev, device_id_type=MESH)

    fx, ub = gf_out, proj_out
    feat_in = pltpu.make_async_copy(feat, fx, in_sem.at[0])
    up_in = pltpu.make_async_copy(up, ub, in_sem.at[1])
    feat_in.start()
    up_in.start()

    wt[y, zh, core] = pwt[...]
    for i in range(3):
        place(wf, i, lambda j: kern[i, j])

    row = lax.broadcasted_iota(jnp.int32, (512, 128), 0) % 64

    feat_in.wait()

    @pl.loop(0, 8)
    def _(k):
        st[8:1032, :] = fx[pl.ds(k * 8, 8)].reshape(1024, 128).astype(F32)
        at = pl.ds(k * 8 + 1, 8)
        x4[at, :, 0:128] = st[pl.ds(8, 512, stride=2), :].astype(BF).reshape(8, 64, 128)
        x4[at, :, 128:256] = st[pl.ds(9, 512, stride=2), :].astype(BF).reshape(8, 64, 128)
        low = jnp.where(row == 0, 0.0, st[pl.ds(7, 512, stride=2), :])
        x4[at, :, 256:384] = low.astype(BF).reshape(8, 64, 128)
        high = jnp.where(row == 63, 0.0, st[pl.ds(10, 512, stride=2), :])
        x4[at, :, 384:512] = high.astype(BF).reshape(8, 64, 128)

    def forward(k):
        t0 = k * 8
        lhs = jnp.concatenate([x4[pl.ds(t0 + i, 8)].reshape(512, 512) for i in range(3)], axis=1)
        pre = dot(lhs, wf[...])
        here = x4[pl.ds(t0 + 1, 8), :, 0:256].reshape(512, 256).astype(F32)
        sig = 0.5 * jnp.tanh(0.5 * pre) + 0.5
        act = pre * sig
        slope = (sig + act * (1.0 - sig)).reshape(4, 2, 64, 256)
        hidden = (here + act).astype(BF).reshape(4, 2, 64, 256)
        at = pl.ds(k * 4, 4)
        both = jnp.concatenate([hidden[:, 0], hidden[:, 1]], axis=-1)
        pk[at] = both
        sl[at, :, 0:256] = slope[:, 0]
        sl[at, :, 256:512] = slope[:, 1]
        pkt[:, pl.ds(pl.multiple_of(k * 256, 256), 256)] = both.reshape(256, 512).T

    @pl.loop(1, EARLY)
    def _(k):
        forward(k)

    pl.semaphore_wait(barrier, len(greet))

    wz = [
        remote(
            wt.at[y, zh, core], wt.at[y, zh, core], wz_s.at[d - 1], wz_r.at[d - 1],
            device(x, y, (z + side * d + 8) % 8, core),
        )
        for d in range(1, 4)
    ]
    for copy in wz:
        copy.start()
    hx = [
        remote(x4.at[1], x4.at[65], hx_s.at[0], hx_r.at[0], left),
        remote(x4.at[64], x4.at[0], hx_s.at[1], hx_r.at[1], right),
    ]
    for copy in hx:
        copy.start()

    @pl.loop(EARLY, 7)
    def _(k):
        forward(k)

    for copy in hx:
        copy.wait()

    @pl.when(tm == 0)
    def _():
        x4[0] = jnp.zeros((64, 512), BF)

    @pl.when(tm == 31)
    def _():
        x4[65] = jnp.zeros((64, 512), BF)

    forward(0)
    forward(7)

    @pl.loop(0, 8)
    def _(k):
        xtb[:, pl.ds(pl.multiple_of(k * 512, 512), 512)] = x4[pl.ds(k * 8 + 1, 8)].reshape(512, 512).T

    for copy in wz:
        copy.wait()
    wy = {
        d: remote(wt.at[y, :, core], wt.at[y, :, core], wy_s.at[d - 1], wy_r.at[d - 1], y_peer(d))
        for d in (1, 3, 2)
    }
    for copy in wy.values():
        copy.start()

    wc = {
        e: remote(
            wt.at[(y + 4 - e) % 4, :, core], wt.at[(y + 4 - e) % 4, :, core],
            wc_s.at[e], wc_r.at[e], partner,
        )
        for e in range(4)
    }

    wc[0].start()

    up_in.wait()
    g0 = [remote(gps.at[1 - core, :, n], r0.at[:, n], g0_s.at[n], g0_r.at[n], partner) for n in range(4)]
    for n in range(4):
        part = dot(pkt[...], ub[:, :, n * 256 : n * 256 + 256].reshape(2048, 256))
        part = part.astype(BF).T.reshape(4, 2, 32, 512)
        for c in range(2):
            for q in range(4):
                gps[c, q, n] = part[:, c, :, q * 128 : q * 128 + 128]
        g0[n].start()

    @pl.loop(0, 8)
    def _(k):
        xta[:, pl.ds(pl.multiple_of(k * 512, 512), 512)] = x4[pl.ds(k * 8, 8)].reshape(512, 512).T

    xta[:, 4096:4224] = x4[64:66].reshape(128, 512).T

    for copy in g0:
        copy.wait()
    s1[...] = (gps[core].astype(F32) + r0[...].astype(F32)).astype(BF)
    g1 = [
        remote(s1.at[(x + d) % 4], r1.at[x], g1_s.at[d - 1], g1_r.at[d - 1], x_peer(d)) for d in (1, 2, 3)
    ]
    for copy in g1:
        copy.start()
    r1[x] = s1[x]

    for e in (1, 3):
        wy[e].wait()
        wc[e].start()
    for e in (0, 1, 3):
        wc[e].wait()

    near = [y, (y + 1) % 4, (y + 3) % 4]
    far = (y + 2) % 4

    def filters(k, n):
        cols = pl.ds(pl.multiple_of(n * 256, 256), 256)
        return ub[pl.ds(k * 8, 8), :, cols].reshape(512, 256)

    @pl.loop(0, 4)
    def _(k):
        lhs = jnp.concatenate([filters(k, n) for n in near], axis=1)
        rhs = jnp.concatenate([wt[n].reshape(256, 512) for n in near], axis=0)
        gh[pl.ds(k * 8, 8)] = dot(lhs, rhs).reshape(8, 64, 512)

    wy[2].wait()
    wc[2].start()
    wc[2].wait()

    def grads(k):
        at = pl.ds(k * 8, 8)
        gp = gh[at].reshape(512, 512) + dot(filters(k, far), wt[far].reshape(256, 512))
        gh[at] = gp.reshape(8, 64, 512)
        g = (gp * sl[at].reshape(512, 512)).astype(BF).reshape(8, 64, 512)
        for t in range(8):
            for p in range(2):
                y4c[k * 16 + 1 + 2 * t + p] = g[t, :, p * 256 : p * 256 + 256]

    @pl.loop(0, 4)
    def _(k):
        grads(k)

    hy = [
        remote(y4c.at[1], y4c.at[65], hy_s.at[0], hy_r.at[0], left),
        remote(y4c.at[64], y4c.at[0], hy_s.at[1], hy_r.at[1], right),
    ]
    for copy in hy:
        copy.start()

    for i in range(3):
        rows = (xta[:, 0:4096], xtb[...], xta[:, 128:4224])[i]
        full = dot(rows, y4c[1:65].reshape(4096, 256))
        at = [[full[128 * n : 128 * n + 128, 128 * q : 128 * q + 128] for q in range(2)] for n in range(4)]
        parts = (at[0][1] + at[2][0], at[0][0] + at[1][1], at[1][0] + at[3][1])
        for j in range(3):
            block = parts[j].astype(BF).reshape(8, 16, 128)
            n = (i * 3 + j) * 8
            if n < 36 < n + 8:
                k0[0, n:36] = block[: 36 - n]
                k0[1, 0 : n - 28] = block[36 - n :]
            else:
                k0[n // 36, n % 36 : n % 36 + 8] = block
    ka = remote(k0.at[1 - core], ra, ka_s.at[0], ka_r.at[0], partner)
    ka.start()

    for copy in g1:
        copy.wait()
    total = r1[0].astype(F32)
    for n in range(1, 4):
        total = total + r1[n].astype(F32)
    s2[...] = total.astype(BF)
    g2 = [
        remote(s2.at[(y + d) % 4], r2.at[y], g2_s.at[d - 1], g2_r.at[d - 1], y_peer(d)) for d in (1, 2, 3)
    ]

    ka.wait()
    sb[0:12] = (k0[core].astype(F32) + ra[...].astype(F32)).astype(BF).reshape(12, 3, 16, 128)
    sb[12:16] = jnp.zeros((4, 3, 16, 128), BF)
    kb = []
    for d in range(1, 16):
        owner = ((x + d // 4) % 4) * 4 + (y + d % 4) % 4
        kb.append(remote(sb.at[owner], rb.at[xy], kb_s.at[d - 1], kb_r.at[d - 1], xy_peer(d)))
    for copy in kb:
        copy.start()
    for copy in g2:
        copy.start()
    rb[xy] = sb[xy]
    r2[y] = s2[y]

    row3 = lax.broadcasted_iota(jnp.int32, (8, 64, 128), 1)

    def widen(at, n):
        c = y4c[at].astype(F32)
        y4w[at, :, 0:128] = jnp.where(row3[:n] == 0, 0.0, pltpu.roll(c[:, :, 128:256], 1, 1)).astype(BF)
        y4w[at, :, 128:256] = jnp.where(row3[:n] == 63, 0.0, pltpu.roll(c[:, :, 0:128], 63, 1)).astype(BF)

    def backward(k):
        t0 = k * 8
        lhs = []
        for i in range(3):
            lhs.append(y4c[pl.ds(t0 + i, 8)].reshape(512, 256))
            lhs.append(y4w[pl.ds(t0 + i, 8)].reshape(512, 256))
        out = dot(jnp.concatenate(lhs, axis=1), wb[...])
        h = gh[pl.ds(k * 4, 4)]
        out = out + jnp.concatenate(
            [h[t, :, p * 256 : p * 256 + 256] for t in range(4) for p in range(2)], axis=0
        )
        st[pl.ds(8, 512, stride=2), :] = out[:, 0:128]
        st[pl.ds(9, 512, stride=2), :] = out[:, 128:256]
        gf_out[pl.ds(t0, 8)] = st[8:1032, :].astype(BF).reshape(8, 128, 128)

    def project(k):
        proj_out[pl.ds(k * 8, 8)] = (
            dot(pk[pl.ds(k * 8, 8)].reshape(512, 512), wn[...]).astype(BF).reshape(8, 64, 1024)
        )

    @pl.loop(0, 8)
    def _(k):
        widen(pl.ds(k * 8 + 1, 8), 8)

    for i in range(3):
        place(wb, i, lambda j: kern[2 - i, 2 - j].T)

    @pl.loop(1, 4)
    def _(k):
        backward(k)

    for copy in kb:
        copy.wait()
    total = rb[0].astype(F32)
    for n in range(1, 16):
        total = total + rb[n].astype(F32)
    sc[...] = total.astype(BF)
    kc = [remote(sc, rc.at[z], kc_s.at[d - 1], kc_r.at[d - 1], z_peer(d)) for d in range(1, 8)]
    for copy in kc:
        copy.start()
    rc[z] = sc[...]

    for copy in g2:
        copy.wait()
    total = r2[0].astype(F32)
    for n in range(1, 4):
        total = total + r2[n].astype(F32)
    s3[...] = total.astype(BF).reshape(4, 2, 16, 128)
    g3 = []
    for d in range(1, 8):
        zd = (z + d) % 8
        g3.append(remote(s3.at[zd // 2, zd % 2], r3.at[z], g3_s.at[d - 1], g3_r.at[d - 1], z_peer(d)))
    for copy in g3:
        copy.start()
    r3[z] = s3[zh, zl]

    for copy in hy:
        copy.wait()

    @pl.when(tm == 0)
    def _():
        y4c[0] = jnp.zeros((64, 256), BF)

    @pl.when(tm == 31)
    def _():
        y4c[65] = jnp.zeros((64, 256), BF)

    widen(pl.ds(0, 1), 1)
    widen(pl.ds(65, 1), 1)
    backward(0)

    @pl.loop(4, 8)
    def _(k):
        backward(k)

    for copy in kc:
        copy.wait()
    total = rc[0].astype(F32)
    for zz in range(1, 8):
        total = total + rc[zz].astype(F32)
    kd[xy] = total.astype(BF)
    kdc = [
        remote(kd.at[xy], kd.at[xy], kd_s.at[d - 1], kd_r.at[d - 1], xy_peer(d)) for d in range(1, 16)
    ]
    for copy in kdc:
        copy.start()

    for copy in g3:
        copy.wait()
    total = r3[0].astype(F32)
    for n in range(1, 8):
        total = total + r3[n].astype(F32)
    r4[bt] = total * scale
    g4 = [remote(r4.at[bt], r4.at[bt], g4_s.at[d - 1], g4_r.at[d - 1], b_peer(d)) for d in range(1, 8)]
    for copy in g4:
        copy.start()

    for yy in range(4):
        wn[:, yy * 256 : (yy + 1) * 256] = wt[yy].reshape(256, 512).T

    @pl.loop(0, 3)
    def _(k):
        project(k)

    for copy in kdc:
        copy.wait()
    kec = remote(kd, ke, ke_s.at[0], ke_r.at[0], partner)
    kec.start()

    project(3)
    for copy in g4:
        copy.wait()
    for n in range(8):
        q, half = n // 2, n % 2
        gp_out[half * 16 : half * 16 + 16, q * 128 : q * 128 + 128] = r4[n]

    gk_out[core] = kd[0:12].astype(F32).reshape(36, 16, 128) * scale
    kec.wait()
    gk_out[1 - core] = ke[0:12].astype(F32).reshape(36, 16, 128) * scale


def vm(*shape, dtype=BF):
    return pltpu.VMEM(shape, dtype)


def write_out(p_in, f_in, k_in, g_in, p_out, f_out, k_out, g_out, sem):
    pairs = [(p_in.at[n * 4 : n * 4 + 4], p_out.at[n * 4 : n * 4 + 4]) for n in range(8)]
    pairs += [(f_in.at[n * 16 : n * 16 + 16], f_out.at[n * 16 : n * 16 + 16]) for n in range(4)]
    pairs += [(k_in, k_out), (g_in, g_out)]
    copies = [pltpu.make_async_copy(a, b, sem.at[n]) for n, (a, b) in enumerate(pairs)]
    for copy in copies:
        copy.start()
    for copy in copies:
        copy.wait()


def body(features, kernel_one, proj_weight, upstream):
    scale = 1.0 / math.sqrt(8 * 2048 * 128)
    dma = pltpu.SemaphoreType.DMA
    counts = [2]
    counts += [2, 2, 2, 2, 3, 3, 3, 3, 4, 4]
    counts += [4, 4, 3, 3, 3, 3, 7, 7, 7, 7]
    counts += [1, 1, 15, 15, 7, 7, 15, 15, 1, 1]
    whole = pl.BlockSpec(memory_space=pltpu.VMEM)
    hbm = pl.BlockSpec(memory_space=pl.ANY)
    projected, grad_features, gk, gp = pl.pallas_call(
        lambda *refs: kernel(scale, *refs),
        out_shape=(
            vm(32, 64, 1024),
            vm(64, 128, 128),
            vm(2, 36, 16, 128, dtype=F32),
            vm(32, 512, dtype=F32),
        ),
        in_specs=[hbm, whole, whole, hbm],
        out_specs=(whole, whole, whole, whole),
        scratch_shapes=[
            vm(1040, 128, dtype=F32),
            vm(66, 64, 512),
            vm(512, 4224),
            vm(512, 4096),
            vm(66, 64, 256),
            vm(66, 64, 256),
            vm(32, 64, 512, dtype=F32),
            vm(32, 64, 512),
            vm(512, 2048),
            vm(32, 64, 512, dtype=F32),
            vm(4, 4, 2, 32, 512),
            vm(512, 1024),
            vm(1536, 256),
            vm(1536, 256),
            vm(2, 4, 4, 4, 32, 128),
            vm(4, 4, 4, 32, 128),
            vm(4, 4, 4, 32, 128),
            vm(4, 4, 4, 32, 128),
            vm(4, 4, 32, 128),
            vm(4, 4, 32, 128),
            vm(4, 2, 16, 128),
            vm(8, 16, 128),
            vm(8, 16, 128, dtype=F32),
            vm(2, 36, 16, 128),
            vm(36, 16, 128),
            vm(16, 3, 16, 128),
            vm(16, 3, 16, 128),
            vm(3, 16, 128),
            vm(8, 3, 16, 128),
            vm(16, 3, 16, 128),
            vm(16, 3, 16, 128),
        ]
        + [dma((n,)) for n in counts],
        compiler_params=pltpu.CompilerParams(
            collective_id=0, has_side_effects=True, vmem_limit_bytes=52 * 1024 * 1024
        ),
    )(features[0], kernel_one, proj_weight.T, upstream[0])
    results = (projected, grad_features, gk, gp)
    projected, grad_features, gk, gp = pl.pallas_call(
        write_out,
        out_shape=tuple(jax.ShapeDtypeStruct(r.shape, r.dtype) for r in results),
        in_specs=[hbm] * 4,
        out_specs=(hbm,) * 4,
        scratch_shapes=[dma((14,))],
        compiler_params=pltpu.CompilerParams(vmem_limit_bytes=1024 * 1024),
    )(*[pltpu.with_memory_space_constraint(r, pltpu.VMEM) for r in results])
    return projected[None], grad_features[None], gk.reshape(3, 3, 128, 128), gp.T


def solution(mesh):
    placed = (P("batch", "tm", None, None), P(), P(None, "tm"), P("batch", "tm", None, None))
    return jax.shard_map(
        body,
        mesh=mesh,
        in_specs=placed,
        out_specs=(P("batch", "tm", None, None), P("batch", "tm", None, None), P(), P(None, "tm")),
        check_vma=False,
    )
```

time: 72.1 us -> 63 us (0.87)
  local copies, waits for them, and re-layouts: 10.7 us -> 0 us
  Pallas kernels: 60.6 us -> 62.1 us
    unnamed x8 -> x0, local copies, waits for them, and re-layouts: 8.54 us -> none
    reshape x1 -> x0, local copies, waits for them, and re-layouts: 2.11 us -> none  [body(): gk.reshape(3, 3, 128, 128)]
    pallas_call x1 -> x2, Pallas kernels: 60.6 us -> 62.1 us  [the longest x1 59.2 us: body(): pl.pallas_call(lambda *refs: kernel(scale, *refs), out_shape=(vm(32, 64,...]
where the time goes in v2:
time: 63 us; the launch traced here: 62.9 us
  Pallas kernels  62.1 us (99%)
  between operations  0.8 us (1%)
    pallas_call x1, Pallas kernels, body(): pl.pallas_call(lambda *refs: kernel(scale, *refs), out_shape=(vm(32, 64,...  59.2 us
    pallas_call x1, Pallas kernels, body(): pl.pallas_call(write_out, out_shape=tuple((jax.ShapeDtypeStruct(r.shape,...  2.95 us

profile of v2, /device:TPU:1, one launch (start us, length us, event | category | flops | bytes accessed | tf_op | source)
XLA Modules:
  0.0 62.9 jit_solution(5199284969532485765)
XLA Ops:
  0.6 59.2 %shard_map.75 = (bf16[32,64,1024]{2,1,0:T(8,128)(2,1)S(1)}, bf16[64,128,128]{2,1,0:T(8,128)(2,1)S(1)}, f32[2,36,16,128]{3,2,1,0:T(8,128)S(1)}, f32[32,512]{1,0:T(8,128)S(1)}) custom-call(bf16[64,128,128]{2,1,0:T(8,128)(2,1)} %bitcast.8, bf16[3,3,128,128]{3,2,1,0:T(8,128)(2,1)} %refs_1_.1, bf16[32,512]{1,0:T(8,128)(2,1)} %bitcast.9, bf16[32,64,1024]{2,1,0:T(8,128)(2,1)} %bitcast.7), custom_call_target="tpu_custom_call" | custom-call | tf_op jit(solution)/shard_map/pallas_call | solution.py:452
  59.8 3.0 %shard_map.76 = (bf16[32,64,1024]{2,1,0:T(8,128)(2,1)}, bf16[64,128,128]{2,1,0:T(8,128)(2,1)}, f32[2,36,16,128]{3,2,1,0:T(8,128)}, f32[32,512]{1,0:T(8,128)}) custom-call(bf16[32,64,1024]{2,1,0:T(8,128)(2,1)S(1)} %get-tuple-element.12.p_in, bf16[64,128,128]{2,1,0:T(8,128)(2,1)S(1)} %get-tuple-element.13.f_in, f32[2,36,16,128]{3,2,1,0:T(8,128)S(1)} %get-tuple-element.14.k_in, ...), custom_call_target="tpu_custom_call" | custom-call | tf_op jit(solution)/shard_map/pallas_call | solution.py:501

commit v3 on v2

--- a/solution.py
+++ b/solution.py
@@ -10,7 +10,7 @@
 BF = jnp.bfloat16
 F32 = jnp.float32
 MESH = pl.DeviceIdType.MESH
-EARLY = 4
+EARLY = 2
 
 
 def dot(a, b):
@@ -31,8 +31,8 @@
 
 
 def kernel(
-    scale, feat, kern, pwt, up, proj_out, gf_out, gk_out, gp_out,
-    st, x4, xta, xtb, y4c, y4w, sl, pk, pkt, gh, wt, wn, wf, wb,
+    scale, feat, kern_in, pwt, up, proj_out, gf_out, gk_out, gp_out,
+    kern, st, fh, x4, xta, xtb, y4c, y4w, sl, pk, pkt, gh, wt, wn, wf, wb,
     gps, r0, s1, r1, s2, r2, s3, r3, r4,
     k0, ra, sb, rb, sc, rc, kd, ke,
     in_sem,
@@ -85,29 +85,48 @@
         pl.semaphore_signal(barrier, inc=1, device_id=dev, device_id_type=MESH)
 
     fx, ub = gf_out, proj_out
-    feat_in = pltpu.make_async_copy(feat, fx, in_sem.at[0])
-    up_in = pltpu.make_async_copy(up, ub, in_sem.at[1])
-    feat_in.start()
-    up_in.start()
-
-    wt[y, zh, core] = pwt[...]
+    feat_in = [
+        pltpu.make_async_copy(
+            feat.at[n * 16 : n * 16 + 16], fx.at[n * 16 : n * 16 + 16], in_sem.at[n]
+        )
+        for n in range(4)
+    ]
+    up_in = [
+        pltpu.make_async_copy(up.at[n * 8 : n * 8 + 8], ub.at[n * 8 : n * 8 + 8], in_sem.at[4 + n])
+        for n in range(4)
+    ]
+    small_in = [
+        pltpu.make_async_copy(kern_in, kern, in_sem.at[8]),
+        pltpu.make_async_copy(pwt, wt.at[y, zh, core], in_sem.at[9]),
+    ]
+    for copy in small_in + feat_in:
+        copy.start()
+    for copy in small_in:
+        copy.wait()
+
     for i in range(3):
         place(wf, i, lambda j: kern[i, j])
 
-    row = lax.broadcasted_iota(jnp.int32, (512, 128), 0) % 64
-
-    feat_in.wait()
+    def build(src, at, frames):
+        count = frames * 64
+        row = lax.broadcasted_iota(jnp.int32, (count, 128), 0) % 64
+        st[8 : 8 + frames * 128, :] = src.reshape(frames * 128, 128).astype(F32)
+        shape = (frames, 64, 128)
+        x4[at, :, 0:128] = st[pl.ds(8, count, stride=2), :].astype(BF).reshape(shape)
+        x4[at, :, 128:256] = st[pl.ds(9, count, stride=2), :].astype(BF).reshape(shape)
+        low = jnp.where(row == 0, 0.0, st[pl.ds(7, count, stride=2), :])
+        x4[at, :, 256:384] = low.astype(BF).reshape(shape)
+        high = jnp.where(row == 63, 0.0, st[pl.ds(10, count, stride=2), :])
+        x4[at, :, 384:512] = high.astype(BF).reshape(shape)
+
+    for copy in feat_in:
+        copy.wait()
+    for copy in up_in:
+        copy.start()
 
     @pl.loop(0, 8)
     def _(k):
-        st[8:1032, :] = fx[pl.ds(k * 8, 8)].reshape(1024, 128).astype(F32)
-        at = pl.ds(k * 8 + 1, 8)
-        x4[at, :, 0:128] = st[pl.ds(8, 512, stride=2), :].astype(BF).reshape(8, 64, 128)
-        x4[at, :, 128:256] = st[pl.ds(9, 512, stride=2), :].astype(BF).reshape(8, 64, 128)
-        low = jnp.where(row == 0, 0.0, st[pl.ds(7, 512, stride=2), :])
-        x4[at, :, 256:384] = low.astype(BF).reshape(8, 64, 128)
-        high = jnp.where(row == 63, 0.0, st[pl.ds(10, 512, stride=2), :])
-        x4[at, :, 384:512] = high.astype(BF).reshape(8, 64, 128)
+        build(fx[pl.ds(k * 8, 8)], pl.ds(k * 8 + 1, 8), 8)
 
     def forward(k):
         t0 = k * 8
@@ -138,46 +157,50 @@
         )
         for d in range(1, 4)
     ]
-    for copy in wz:
-        copy.start()
-    hx = [
-        remote(x4.at[1], x4.at[65], hx_s.at[0], hx_r.at[0], left),
-        remote(x4.at[64], x4.at[0], hx_s.at[1], hx_r.at[1], right),
-    ]
-    for copy in hx:
-        copy.start()
-
-    @pl.loop(EARLY, 7)
-    def _(k):
-        forward(k)
-
-    for copy in hx:
-        copy.wait()
-
-    @pl.when(tm == 0)
-    def _():
-        x4[0] = jnp.zeros((64, 512), BF)
-
-    @pl.when(tm == 31)
-    def _():
-        x4[65] = jnp.zeros((64, 512), BF)
-
-    forward(0)
-    forward(7)
-
-    @pl.loop(0, 8)
-    def _(k):
-        xtb[:, pl.ds(pl.multiple_of(k * 512, 512), 512)] = x4[pl.ds(k * 8 + 1, 8)].reshape(512, 512).T
-
-    for copy in wz:
-        copy.wait()
+    turn = [zh, (zh + side + 4) % 4, (zh - side + 4) % 4, (zh + 2) % 4]
     wy = {
-        d: remote(wt.at[y, :, core], wt.at[y, :, core], wy_s.at[d - 1], wy_r.at[d - 1], y_peer(d))
+        (n, d): remote(
+            wt.at[y, turn[n], core], wt.at[y, turn[n], core],
+            wy_s.at[n * 4 + d], wy_r.at[n * 4 + d], y_peer(d),
+        )
+        for n in range(4)
         for d in (1, 3, 2)
     }
-    for copy in wy.values():
-        copy.start()
-
+
+    def along_y(n):
+        if n > 0:
+            wz[n - 1].wait()
+        for d in (1, 3, 2):
+            wy[n, d].start()
+
+    for copy in wz:
+        copy.start()
+    along_y(0)
+    hx = [
+        remote(fx.at[0], fh.at[1], hx_s.at[0], hx_r.at[0], left),
+        remote(fx.at[63], fh.at[0], hx_s.at[1], hx_r.at[1], right),
+    ]
+
+    for copy in hx:
+        copy.start()
+
+    @pl.loop(EARLY, 7)
+    def _(k):
+        forward(k)
+
+    along_y(1)
+
+    @pl.loop(0, 8)
+    def _(k):
+        xtb[:, pl.ds(pl.multiple_of(k * 512, 512), 512)] = x4[pl.ds(k * 8 + 1, 8)].reshape(512, 512).T
+
+    along_y(2)
+
+    @pl.loop(1, 5)
+    def _(k):
+        xta[:, pl.ds(pl.multiple_of(k * 512, 512), 512)] = x4[pl.ds(k * 8, 8)].reshape(512, 512).T
+
+    along_y(3)
     wc = {
         e: remote(
             wt.at[(y + 4 - e) % 4, :, core], wt.at[(y + 4 - e) % 4, :, core],
@@ -185,11 +208,41 @@
         )
         for e in range(4)
     }
-
     wc[0].start()
-
-    up_in.wait()
+    for copy in hx:
+        copy.wait()
+
+    @pl.when(tm == 0)
+    def _():
+        fh[0] = jnp.zeros((128, 128), BF)
+
+    @pl.when(tm == 31)
+    def _():
+        fh[1] = jnp.zeros((128, 128), BF)
+
+    build(fh[0:1], pl.ds(0, 1), 1)
+    build(fh[1:2], pl.ds(65, 1), 1)
+    forward(0)
+    forward(7)
+
+    for copy in up_in:
+        copy.wait()
     g0 = [remote(gps.at[1 - core, :, n], r0.at[:, n], g0_s.at[n], g0_r.at[n], partner) for n in range(4)]
+    g1 = {
+        (n, d): remote(
+            s1.at[(x + d) % 4, n], r1.at[x, n], g1_s.at[n * 4 + d], g1_r.at[n * 4 + d], x_peer(d)
+        )
+        for n in range(4)
+        for d in (1, 3, 2)
+    }
+
+    def core_sum(n):
+        g0[n].wait()
+        s1[:, n] = (gps[core, :, n].astype(F32) + r0[:, n].astype(F32)).astype(BF)
+        for d in (1, 3, 2):
+            g1[n, d].start()
+        r1[x, n] = s1[x, n]
+
     for n in range(4):
         part = dot(pkt[...], ub[:, :, n * 256 : n * 256 + 256].reshape(2048, 256))
         part = part.astype(BF).T.reshape(4, 2, 32, 512)
@@ -197,58 +250,35 @@
             for q in range(4):
                 gps[c, q, n] = part[:, c, :, q * 128 : q * 128 + 128]
         g0[n].start()
-
-    @pl.loop(0, 8)
+        if n > 1:
+            core_sum(n - 2)
+
+    for e in (1, 3, 2):
+        for n in range(4):
+            wy[n, e].wait()
+        wc[e].start()
+    core_sum(2)
+    core_sum(3)
+
+    @pl.loop(5, 8)
     def _(k):
         xta[:, pl.ds(pl.multiple_of(k * 512, 512), 512)] = x4[pl.ds(k * 8, 8)].reshape(512, 512).T
 
+    xta[:, 0:512] = x4[0:8].reshape(512, 512).T
     xta[:, 4096:4224] = x4[64:66].reshape(128, 512).T
 
-    for copy in g0:
-        copy.wait()
-    s1[...] = (gps[core].astype(F32) + r0[...].astype(F32)).astype(BF)
-    g1 = [
-        remote(s1.at[(x + d) % 4], r1.at[x], g1_s.at[d - 1], g1_r.at[d - 1], x_peer(d)) for d in (1, 2, 3)
-    ]
-    for copy in g1:
-        copy.start()
-    r1[x] = s1[x]
-
-    for e in (1, 3):
-        wy[e].wait()
-        wc[e].start()
-    for e in (0, 1, 3):
-        wc[e].wait()
-
-    near = [y, (y + 1) % 4, (y + 3) % 4]
-    far = (y + 2) % 4
-
-    def filters(k, n):
-        cols = pl.ds(pl.multiple_of(n * 256, 256), 256)
-        return ub[pl.ds(k * 8, 8), :, cols].reshape(512, 256)
-
-    @pl.loop(0, 4)
-    def _(k):
-        lhs = jnp.concatenate([filters(k, n) for n in near], axis=1)
-        rhs = jnp.concatenate([wt[n].reshape(256, 512) for n in near], axis=0)
-        gh[pl.ds(k * 8, 8)] = dot(lhs, rhs).reshape(8, 64, 512)
-
-    wy[2].wait()
-    wc[2].start()
-    wc[2].wait()
-
-    def grads(k):
+    for copy in wc.values():
+        copy.wait()
+
+    @pl.loop(0, 4, unroll=True)
+    def _(k):
         at = pl.ds(k * 8, 8)
-        gp = gh[at].reshape(512, 512) + dot(filters(k, far), wt[far].reshape(256, 512))
+        gp = dot(ub[at].reshape(512, 1024), wt[...].reshape(1024, 512))
         gh[at] = gp.reshape(8, 64, 512)
         g = (gp * sl[at].reshape(512, 512)).astype(BF).reshape(8, 64, 512)
         for t in range(8):
             for p in range(2):
                 y4c[k * 16 + 1 + 2 * t + p] = g[t, :, p * 256 : p * 256 + 256]
-
-    @pl.loop(0, 4)
-    def _(k):
-        grads(k)
 
     hy = [
         remote(y4c.at[1], y4c.at[65], hy_s.at[0], hy_r.at[0], left),
@@ -273,7 +303,7 @@
     ka = remote(k0.at[1 - core], ra, ka_s.at[0], ka_r.at[0], partner)
     ka.start()
 
-    for copy in g1:
+    for copy in g1.values():
         copy.wait()
     total = r1[0].astype(F32)
     for n in range(1, 4):
@@ -282,6 +312,9 @@
     g2 = [
         remote(s2.at[(y + d) % 4], r2.at[y], g2_s.at[d - 1], g2_r.at[d - 1], y_peer(d)) for d in (1, 2, 3)
     ]
+    for copy in g2:
+        copy.start()
+    r2[y] = s2[y]
 
     ka.wait()
     sb[0:12] = (k0[core].astype(F32) + ra[...].astype(F32)).astype(BF).reshape(12, 3, 16, 128)
@@ -292,10 +325,7 @@
         kb.append(remote(sb.at[owner], rb.at[xy], kb_s.at[d - 1], kb_r.at[d - 1], xy_peer(d)))
     for copy in kb:
         copy.start()
-    for copy in g2:
-        copy.start()
     rb[xy] = sb[xy]
-    r2[y] = s2[y]
 
     row3 = lax.broadcasted_iota(jnp.int32, (8, 64, 128), 1)
 
@@ -328,24 +358,6 @@
     def _(k):
         widen(pl.ds(k * 8 + 1, 8), 8)
 
-    for i in range(3):
-        place(wb, i, lambda j: kern[2 - i, 2 - j].T)
-
-    @pl.loop(1, 4)
-    def _(k):
-        backward(k)
-
-    for copy in kb:
-        copy.wait()
-    total = rb[0].astype(F32)
-    for n in range(1, 16):
-        total = total + rb[n].astype(F32)
-    sc[...] = total.astype(BF)
-    kc = [remote(sc, rc.at[z], kc_s.at[d - 1], kc_r.at[d - 1], z_peer(d)) for d in range(1, 8)]
-    for copy in kc:
-        copy.start()
-    rc[z] = sc[...]
-
     for copy in g2:
         copy.wait()
     total = r2[0].astype(F32)
@@ -360,6 +372,24 @@
         copy.start()
     r3[z] = s3[zh, zl]
 
+    for i in range(3):
+        place(wb, i, lambda j: kern[2 - i, 2 - j].T)
+
+    @pl.loop(1, 4)
+    def _(k):
+        backward(k)
+
+    for copy in kb:
+        copy.wait()
+    total = rb[0].astype(F32)
+    for n in range(1, 16):
+        total = total + rb[n].astype(F32)
+    sc[...] = total.astype(BF)
+    kc = [remote(sc, rc.at[z], kc_s.at[d - 1], kc_r.at[d - 1], z_peer(d)) for d in range(1, 8)]
+    for copy in kc:
+        copy.start()
+    rc[z] = sc[...]
+
     for copy in hy:
         copy.wait()
 
@@ -370,6 +400,16 @@
     @pl.when(tm == 31)
     def _():
         y4c[65] = jnp.zeros((64, 256), BF)
+
+    for copy in g3:
+        copy.wait()
+    total = r3[0].astype(F32)
+    for n in range(1, 8):
+        total = total + r3[n].astype(F32)
+    r4[bt] = total * scale
+    g4 = [remote(r4.at[bt], r4.at[bt], g4_s.at[d - 1], g4_r.at[d - 1], b_peer(d)) for d in range(1, 8)]
+    for copy in g4:
+        copy.start()
 
     widen(pl.ds(0, 1), 1)
     widen(pl.ds(65, 1), 1)
@@ -391,16 +431,6 @@
     for copy in kdc:
         copy.start()
 
-    for copy in g3:
-        copy.wait()
-    total = r3[0].astype(F32)
-    for n in range(1, 8):
-        total = total + r3[n].astype(F32)
-    r4[bt] = total * scale
-    g4 = [remote(r4.at[bt], r4.at[bt], g4_s.at[d - 1], g4_r.at[d - 1], b_peer(d)) for d in range(1, 8)]
-    for copy in g4:
-        copy.start()
-
     for yy in range(4):
         wn[:, yy * 256 : (yy + 1) * 256] = wt[yy].reshape(256, 512).T
 
@@ -443,9 +473,9 @@
 def body(features, kernel_one, proj_weight, upstream):
     scale = 1.0 / math.sqrt(8 * 2048 * 128)
     dma = pltpu.SemaphoreType.DMA
-    counts = [2]
-    counts += [2, 2, 2, 2, 3, 3, 3, 3, 4, 4]
-    counts += [4, 4, 3, 3, 3, 3, 7, 7, 7, 7]
+    counts = [10]
+    counts += [2, 2, 2, 2, 3, 3, 16, 16, 4, 4]
+    counts += [4, 4, 16, 16, 3, 3, 7, 7, 7, 7]
     counts += [1, 1, 15, 15, 7, 7, 15, 15, 1, 1]
     whole = pl.BlockSpec(memory_space=pltpu.VMEM)
     hbm = pl.BlockSpec(memory_space=pl.ANY)
@@ -457,10 +487,12 @@
             vm(2, 36, 16, 128, dtype=F32),
             vm(32, 512, dtype=F32),
         ),
-        in_specs=[hbm, whole, whole, hbm],
+        in_specs=[hbm] * 4,
         out_specs=(whole, whole, whole, whole),
         scratch_shapes=[
+            vm(3, 3, 128, 128),
             vm(1040, 128, dtype=F32),
+            vm(2, 128, 128),
             vm(66, 64, 512),
             vm(512, 4224),
             vm(512, 4096),

time: 63 us -> 59.5 us (0.944)
  Pallas kernels: 62.1 us -> 58.6 us
    pallas_call x1, Pallas kernels: 59.2 us -> 55.6 us  [body(): pl.pallas_call(lambda *refs: kernel(scale, *refs), out_shape=(vm(32, 64,...]
where the time goes in v3:
time: 59.5 us; the launch traced here: 59.4 us
  Pallas kernels  58.6 us (98%)
  between operations  0.8 us (1%)
    pallas_call x1, Pallas kernels, body(): pl.pallas_call(lambda *refs: kernel(scale, *refs), out_shape=(vm(32, 64,...  55.6 us
    pallas_call x1, Pallas kernels, body(): pl.pallas_call(write_out, out_shape=tuple((jax.ShapeDtypeStruct(r.shape,...  2.95 us

profile of v3, /device:TPU:1, one launch (start us, length us, event | category | flops | bytes accessed | tf_op | source)
XLA Modules:
  0.0 59.4 jit_solution(5117406806176675205)
XLA Ops:
  0.6 55.6 %shard_map.75 = (bf16[32,64,1024]{2,1,0:T(8,128)(2,1)S(1)}, bf16[64,128,128]{2,1,0:T(8,128)(2,1)S(1)}, f32[2,36,16,128]{3,2,1,0:T(8,128)S(1)}, f32[32,512]{1,0:T(8,128)S(1)}) custom-call(bf16[64,128,128]{2,1,0:T(8,128)(2,1)} %bitcast.8, bf16[3,3,128,128]{3,2,1,0:T(8,128)(2,1)} %refs_1_.1, bf16[32,512]{1,0:T(8,128)(2,1)} %bitcast.9, bf16[32,64,1024]{2,1,0:T(8,128)(2,1)} %bitcast.7), custom_call_target="tpu_custom_call" | custom-call | tf_op jit(solution)/shard_map/pallas_call | solution.py:482
  56.3 3.0 %shard_map.76 = (bf16[32,64,1024]{2,1,0:T(8,128)(2,1)}, bf16[64,128,128]{2,1,0:T(8,128)(2,1)}, f32[2,36,16,128]{3,2,1,0:T(8,128)}, f32[32,512]{1,0:T(8,128)}) custom-call(bf16[32,64,1024]{2,1,0:T(8,128)(2,1)S(1)} %get-tuple-element.12.p_in, bf16[64,128,128]{2,1,0:T(8,128)(2,1)S(1)} %get-tuple-element.13.f_in, f32[2,36,16,128]{3,2,1,0:T(8,128)S(1)} %get-tuple-element.14.k_in, ...), custom_call_target="tpu_custom_call" | custom-call | tf_op jit(solution)/shard_map/pallas_call | solution.py:533

commit v4 on v3

--- a/solution.py
+++ b/solution.py
@@ -303,19 +303,6 @@
     ka = remote(k0.at[1 - core], ra, ka_s.at[0], ka_r.at[0], partner)
     ka.start()
 
-    for copy in g1.values():
-        copy.wait()
-    total = r1[0].astype(F32)
-    for n in range(1, 4):
-        total = total + r1[n].astype(F32)
-    s2[...] = total.astype(BF)
-    g2 = [
-        remote(s2.at[(y + d) % 4], r2.at[y], g2_s.at[d - 1], g2_r.at[d - 1], y_peer(d)) for d in (1, 2, 3)
-    ]
-    for copy in g2:
-        copy.start()
-    r2[y] = s2[y]
-
     ka.wait()
     sb[0:12] = (k0[core].astype(F32) + ra[...].astype(F32)).astype(BF).reshape(12, 3, 16, 128)
     sb[12:16] = jnp.zeros((4, 3, 16, 128), BF)
@@ -326,6 +313,19 @@
     for copy in kb:
         copy.start()
     rb[xy] = sb[xy]
+
+    for copy in g1.values():
+        copy.wait()
+    total = r1[0].astype(F32)
+    for n in range(1, 4):
+        total = total + r1[n].astype(F32)
+    s2[...] = total.astype(BF)
+    g2 = [
+        remote(s2.at[(y + d) % 4], r2.at[y], g2_s.at[d - 1], g2_r.at[d - 1], y_peer(d)) for d in (1, 2, 3)
+    ]
+    for copy in g2:
+        copy.start()
+    r2[y] = s2[y]
 
     row3 = lax.broadcasted_iota(jnp.int32, (8, 64, 128), 1)
 
@@ -358,6 +358,24 @@
     def _(k):
         widen(pl.ds(k * 8 + 1, 8), 8)
 
+    for i in range(3):
+        place(wb, i, lambda j: kern[2 - i, 2 - j].T)
+
+    @pl.loop(1, 3)
+    def _(k):
+        backward(k)
+
+    for copy in kb:
+        copy.wait()
+    total = rb[0].astype(F32)
+    for n in range(1, 16):
+        total = total + rb[n].astype(F32)
+    sc[...] = total.astype(BF)
+    kc = [remote(sc, rc.at[z], kc_s.at[d - 1], kc_r.at[d - 1], z_peer(d)) for d in range(1, 8)]
+    for copy in kc:
+        copy.start()
+    rc[z] = sc[...]
+
     for copy in g2:
         copy.wait()
     total = r2[0].astype(F32)
@@ -372,24 +390,6 @@
         copy.start()
     r3[z] = s3[zh, zl]
 
-    for i in range(3):
-        place(wb, i, lambda j: kern[2 - i, 2 - j].T)
-
-    @pl.loop(1, 4)
-    def _(k):
-        backward(k)
-
-    for copy in kb:
-        copy.wait()
-    total = rb[0].astype(F32)
-    for n in range(1, 16):
-        total = total + rb[n].astype(F32)
-    sc[...] = total.astype(BF)
-    kc = [remote(sc, rc.at[z], kc_s.at[d - 1], kc_r.at[d - 1], z_peer(d)) for d in range(1, 8)]
-    for copy in kc:
-        copy.start()
-    rc[z] = sc[...]
-
     for copy in hy:
         copy.wait()
 
@@ -400,6 +400,26 @@
     @pl.when(tm == 31)
     def _():
         y4c[65] = jnp.zeros((64, 256), BF)
+
+    widen(pl.ds(0, 1), 1)
+    widen(pl.ds(65, 1), 1)
+    backward(0)
+
+    @pl.loop(3, 6)
+    def _(k):
+        backward(k)
+
+    for copy in kc:
+        copy.wait()
+    total = rc[0].astype(F32)
+    for zz in range(1, 8):
+        total = total + rc[zz].astype(F32)
+    kd[xy] = total.astype(BF)
+    kdc = [
+        remote(kd.at[xy], kd.at[xy], kd_s.at[d - 1], kd_r.at[d - 1], xy_peer(d)) for d in range(1, 16)
+    ]
+    for copy in kdc:
+        copy.start()
 
     for copy in g3:
         copy.wait()
@@ -411,25 +431,9 @@
     for copy in g4:
         copy.start()
 
-    widen(pl.ds(0, 1), 1)
-    widen(pl.ds(65, 1), 1)
-    backward(0)
-
-    @pl.loop(4, 8)
+    @pl.loop(6, 8)
     def _(k):
         backward(k)
-
-    for copy in kc:
-        copy.wait()
-    total = rc[0].astype(F32)
-    for zz in range(1, 8):
-        total = total + rc[zz].astype(F32)
-    kd[xy] = total.astype(BF)
-    kdc = [
-        remote(kd.at[xy], kd.at[xy], kd_s.at[d - 1], kd_r.at[d - 1], xy_peer(d)) for d in range(1, 16)
-    ]
-    for copy in kdc:
-        copy.start()
 
     for yy in range(4):
         wn[:, yy * 256 : (yy + 1) * 256] = wt[yy].reshape(256, 512).T

time: 59.5 us -> 58.7 us (0.987)
  Pallas kernels: 58.6 us -> 57.8 us
    pallas_call x1, Pallas kernels: 55.6 us -> 54.8 us  [body(): pl.pallas_call(lambda *refs: kernel(scale, *refs), out_shape=(vm(32, 64,...]
where the time goes in v4:
time: 58.7 us; the launch traced here: 58.6 us
  Pallas kernels  57.8 us (98%)
  between operations  0.8 us (1%)
    pallas_call x1, Pallas kernels, body(): pl.pallas_call(lambda *refs: kernel(scale, *refs), out_shape=(vm(32, 64,...  54.8 us
    pallas_call x1, Pallas kernels, body(): pl.pallas_call(write_out, out_shape=tuple((jax.ShapeDtypeStruct(r.shape,...  2.95 us

profile of v4, /device:TPU:1, one launch (start us, length us, event | category | flops | bytes accessed | tf_op | source)
XLA Modules:
  0.0 58.6 jit_solution(11126938946892024121)
XLA Ops:
  0.6 54.8 %shard_map.75 = (bf16[32,64,1024]{2,1,0:T(8,128)(2,1)S(1)}, bf16[64,128,128]{2,1,0:T(8,128)(2,1)S(1)}, f32[2,36,16,128]{3,2,1,0:T(8,128)S(1)}, f32[32,512]{1,0:T(8,128)S(1)}) custom-call(bf16[64,128,128]{2,1,0:T(8,128)(2,1)} %bitcast.8, bf16[3,3,128,128]{3,2,1,0:T(8,128)(2,1)} %refs_1_.1, bf16[32,512]{1,0:T(8,128)(2,1)} %bitcast.9, bf16[32,64,1024]{2,1,0:T(8,128)(2,1)} %bitcast.7), custom_call_target="tpu_custom_call" | custom-call | tf_op jit(solution)/shard_map/pallas_call | solution.py:486
  55.5 3.0 %shard_map.76 = (bf16[32,64,1024]{2,1,0:T(8,128)(2,1)}, bf16[64,128,128]{2,1,0:T(8,128)(2,1)}, f32[2,36,16,128]{3,2,1,0:T(8,128)}, f32[32,512]{1,0:T(8,128)}) custom-call(bf16[32,64,1024]{2,1,0:T(8,128)(2,1)S(1)} %get-tuple-element.12.p_in, bf16[64,128,128]{2,1,0:T(8,128)(2,1)S(1)} %get-tuple-element.13.f_in, f32[2,36,16,128]{3,2,1,0:T(8,128)S(1)} %get-tuple-element.14.k_in, ...), custom_call_target="tpu_custom_call" | custom-call | tf_op jit(solution)/shard_map/pallas_call | solution.py:537
